TPU v7x, 32 devices: a whole 2x2x4 slice. The times are simulated.
32 devices in a mesh: prow: 8 (over z, x), pcol: 4 (over y, core).
Axes of the slice: x: 2, y: 2, z: 4, core: 2. Of those that a mesh axis runs over, the one named last changes fastest.
Arguments:
- right_hand_blocks: float32 [8, 4, 512, 256], P('prow'), may hold values from -6 to 6
- diag_inverse: bfloat16 [8, 4, 512, 512], P('prow'), as said below
- lower_blocks: bfloat16 [8, 4, 3, 5, 512, 512], P('prow', 'pcol'), may hold values from -0.0625 to 0.0625
- block_source: int32 [8, 4, 3, 5], P('prow', 'pcol'), may hold values from 0 to 1, as said below
- target_level_per_slot: int32 [8, 4, 3, 5], P('prow', 'pcol'), may hold values from 1 to 4, as said below
Outputs:
- solved: bfloat16 [8, 4, 512, 256], P('prow')
Inputs may be any that keep to these rules, and one draw needn't show every extreme that they name: `target_level_per_slot`: block (source k, target level t) appears at most once among the slots of one device and one source level l; every target level exceeds l; the filled slots come first, and there are min(5, 2 * (3 - l)) of them. `block_source`: an empty slot has source 0. `diag_inverse`: lower triangular, diagonal between 0.5 and 1.5.
All inputs are finite; a program needn't handle non-finite values.
Results may differ from a plain program's by a relative error of at most 0.0075.
Values may be sent and summed in bfloat16 or wider, within the bound.
A program may use at most 128 MiB of HBM per device.

v0:
```python
import jax
import jax.numpy as jnp
from jax import lax
from jax.sharding import PartitionSpec as P


def on_device(right_hand_blocks, diag_inverse, lower_blocks, block_source, target_level_per_slot):
    col_count = lax.axis_size("pcol")
    row_count = lax.axis_size("prow")
    per_col = row_count // col_count
    column = lax.axis_index("pcol")
    levels = right_hand_blocks.shape[1]
    block_width = right_hand_blocks.shape[2]
    rhs_cols = right_hand_blocks.shape[3]
    partial_value = jnp.zeros((levels, block_width, rhs_cols), jnp.float32)
    outputs = []
    for tree_level in range(levels):
        inverse = diag_inverse[0, tree_level]
        given_rhs = right_hand_blocks[0, tree_level]
        if tree_level == 0:
            solved = jnp.dot(
                inverse, given_rhs.astype(jnp.bfloat16), preferred_element_type=jnp.float32
            ).astype(jnp.bfloat16)
        else:
            summed = lax.psum(partial_value[tree_level], "pcol")
            solved = jnp.dot(
                inverse,
                (given_rhs - summed).astype(jnp.bfloat16),
                preferred_element_type=jnp.float32,
            ).astype(jnp.bfloat16)
        outputs.append(solved)
        if tree_level < levels - 1:
            gathered = lax.all_gather(solved, "prow", axis=0, tiled=True)
            gathered = gathered.reshape(per_col, col_count, block_width, rhs_cols)
            by_slot = lax.dynamic_index_in_dim(gathered, column, 1, keepdims=False)
            sources = block_source[0, 0, tree_level]
            targets = target_level_per_slot[0, 0, tree_level]
            picked = jnp.take(by_slot, sources, axis=0)
            block_products = jnp.einsum(
                "bij,bjr->bir",
                lower_blocks[0, 0, tree_level],
                picked,
                preferred_element_type=jnp.float32,
            )
            indicator_matrix = (
                targets[None, :] == jnp.arange(levels, dtype=jnp.int32)[:, None]
            ).astype(jnp.float32)
            partial_value = partial_value + jnp.einsum(
                "tk,kxz->txz", indicator_matrix, block_products, precision=lax.Precision.HIGHEST
            )
    return jnp.stack(outputs, axis=0)[None]


def solution(mesh):
    placed = (
        P("prow", None, None, None),
        P("prow", None, None, None),
        P("prow", "pcol", None, None, None, None),
        P("prow", "pcol", None, None),
        P("prow", "pcol", None, None),
    )
    return jax.shard_map(
        on_device,
        mesh=mesh,
        in_specs=placed,
        out_specs=P("prow", None, None, None),
        check_vma=False,
    )
```

profile of v0, /device:TPU:0, one launch (start us, length us, event | category | flops | bytes accessed | tf_op | source)
XLA Modules:
  0.0 322.7 jit_solution(16675195253927854351)
XLA Ops:
  6.5 0.0 all-gather.4.cloned.1.call-start
  6.5 2.2 convolution_convert_fusion.3
  8.8 0.0 all-gather.4.cloned.1.call-update
  8.8 0.0 all-reduce.4.cloned.1.call-start
  8.8 0.7 compare_and_fusion
  9.5 0.7 slice_bitcast_fusion
  10.2 51.3 %all-gather.4.cloned.1.call-done = bf16[4096,256]{1,0:T(8,128)(2,1)} async-done(((bf16[512,256]{1,0:T(8,128)(2,1)}), bf16[4096,256]{1,0:T(8,128)(2,1)}) %all-gather.4.cloned.1.call-update) | async-done | bytes 2097168 | tf_op jit(solution)/shard_map/all_gather | solution.py:33
  61.5 1.1 dynamic-slice_bitcast_fusion.2
  62.6 1.8 gather_fusion
  64.4 3.2 fusion.10
  67.5 3.5 %copy.9 = f32[5,256,512]{1,0,2:T(8,128)} copy(f32[5,256,512]{2,1,0:T(8,128)S(1)} %fusion.10) | data formatting | bytes 5242880 | tf_op jit(solution)/shard_map/bij,bjr->bir/dot_general | solution.py:39
  71.0 4.2 %fusion.4 = f32[4,512,256]{2,0,1:T(4,128)S(1)} fusion(f32[5,256,512]{1,0,2:T(8,128)} %copy.9, s32[5]{0:T(128)S(1)} %get-tuple-element.13), kind=kOutput, calls=%fused_computation.7 | convolution fusion | flops 31457300 | bytes 4718612 | tf_op jit(solution)/shard_map/tk,kxz->txz/dot_general | solution.py:48
  75.3 0.5 slice.88
  75.8 0.8 copy.23
  76.7 0.0 all-reduce.4.cloned.1.call-update
  76.7 0.0 all-gather.6.cloned.1.call-start
  76.7 31.8 %all-reduce.4.cloned.1.call-done = f32[512,256]{1,0:T(8,128)} async-done(((f32[512,256]{1,0:T(8,128)}), f32[512,256]{1,0:T(8,128)}) %all-reduce.4.cloned.1.call-update) | async-done | bytes 524304 | tf_op jit(solution)/shard_map/psum | solution.py:25
  108.5 2.4 convolution_convert_fusion.2
  110.9 0.0 all-gather.6.cloned.1.call-update
  110.9 0.0 all-reduce.6.cloned.1.call-start
  111.0 49.4 %all-gather.6.cloned.1.call-done = bf16[4096,256]{1,0:T(8,128)(2,1)} async-done(((bf16[512,256]{1,0:T(8,128)(2,1)}), bf16[4096,256]{1,0:T(8,128)(2,1)}) %all-gather.6.cloned.1.call-update) | async-done | bytes 2097168 | tf_op jit(solution)/shard_map/all_gather | solution.py:33
  160.4 1.1 dynamic-slice_bitcast_fusion.1
  161.4 1.8 gather_fusion.1
  163.2 4.7 %fusion.8 = f32[5,256,512]{2,1,0:T(8,128)} fusion(bf16[1,1,3,5,512,512]{5,4,3,2,1,0:T(8,128)(2,1)} %param.9, bf16[5,512,256]{2,1,0:T(8,128)(2,1)} %gather_fusion.1, pred[5]{0:T(512)(128)(4,1)S(1)} %get-tuple-element.17), kind=kOutput, calls=%fused_computation.11 | convolution fusion | flops 671744000 | bytes 6553605 | tf_op jit(solution)/shard_map/bij,bjr->bir/dot_general | solution.py:39
  167.9 5.0 %copy.11 = f32[5,256,512]{1,0,2:T(8,128)} copy(f32[5,256,512]{2,1,0:T(8,128)} %fusion.8) | data formatting | bytes 5242880 | tf_op jit(solution)/shard_map/bij,bjr->bir/dot_general | solution.py:39
  172.9 4.4 %fusion.15 = f32[4,512,256]{2,0,1:T(4,128)S(1)} fusion(f32[4,512,256]{2,0,1:T(4,128)S(1)} %fusion.4, f32[5,256,512]{1,0,2:T(8,128)} %copy.11, s32[5]{0:T(128)S(1)} %get-tuple-element.14), kind=kOutput, calls=%fused_computation.18 | convolution fusion | flops 31981588 | bytes 6815764 | tf_op jit(solution)/shard_map/tk,kxz->txz/dot_general | solution.py:48
  177.3 0.0 copy-start
  177.3 1.3 copy-done
  178.7 0.5 slice.89
  179.2 0.8 copy.22
  180.0 0.0 all-reduce.6.cloned.1.call-update
  180.1 0.0 all-gather.8.cloned.1.call-start
  180.1 31.8 %all-reduce.6.cloned.1.call-done = f32[512,256]{1,0:T(8,128)} async-done(((f32[512,256]{1,0:T(8,128)}), f32[512,256]{1,0:T(8,128)}) %all-reduce.6.cloned.1.call-update) | async-done | bytes 524304 | tf_op jit(solution)/shard_map/psum | solution.py:25
  211.9 2.4 convolution_convert_fusion.1
  214.3 0.0 all-gather.8.cloned.1.call-update
  214.3 0.2 all-reduce.8.cloned.1.call-start
  214.6 49.2 %all-gather.8.cloned.1.call-done = bf16[4096,256]{1,0:T(8,128)(2,1)} async-done(((bf16[512,256]{1,0:T(8,128)(2,1)}), bf16[4096,256]{1,0:T(8,128)(2,1)}) %all-gather.8.cloned.1.call-update) | async-done | bytes 2097168 | tf_op jit(solution)/shard_map/all_gather | solution.py:33
  263.8 1.1 dynamic-slice_bitcast_fusion
  264.8 1.8 gather_fusion.2
  266.6 3.2 fusion.6
  269.8 3.5 %copy.13 = f32[5,256,512]{1,0,2:T(8,128)} copy(f32[5,256,512]{2,1,0:T(8,128)S(1)} %fusion.6) | data formatting | bytes 5242880 | tf_op jit(solution)/shard_map/bij,bjr->bir/dot_general | solution.py:39
  273.3 4.2 %fusion = f32[4,512,256]{2,0,1:T(4,128)S(1)} fusion(f32[5,256,512]{1,0,2:T(8,128)} %copy.13, s32[5]{0:T(128)S(1)} %get-tuple-element.12), kind=kOutput, calls=%fused_computation.3 | convolution fusion | flops 31457300 | bytes 4718612 | tf_op jit(solution)/shard_map/tk,kxz->txz/dot_general | solution.py:48
  277.5 2.8 slice_add_fusion
  280.3 0.0 copy-start.1
  280.4 0.0 copy-start.2
  280.4 0.0 copy-start.3
  280.4 0.8 copy.21
  281.2 0.0 all-reduce.8.cloned.1.call-update
  281.2 31.9 %all-reduce.8.cloned.1.call-done = f32[512,256]{1,0:T(8,128)} async-done(((f32[512,256]{1,0:T(8,128)}), f32[512,256]{1,0:T(8,128)}) %all-reduce.8.cloned.1.call-update) | async-done | bytes 524304 | tf_op jit(solution)/shard_map/psum | solution.py:25
  313.1 1.7 fusion.24
  314.8 0.0 copy-done.1
  314.8 0.0 copy-done.2
  314.8 0.0 copy-done.3
  314.8 1.1 maximum_bitcast_fusion
  (3 shorter events, 0.0 us)
Async XLA Ops:
  6.5 55.0 %all-gather.4.cloned.1.call-start = ((), (), s32[]{:S(2)}) async-start(), calls=%async_computation | async-start | bytes 2359296 | tf_op jit(solution)/shard_map/all_gather | solution.py:33
  8.8 99.8 %all-reduce.4.cloned.1.call-start = ((), (), s32[]{:S(2)}) async-start(), calls=%async_computation.1 | async-start | bytes 1048576 | tf_op jit(solution)/shard_map/psum | solution.py:25
  76.7 83.7 %all-gather.6.cloned.1.call-start = ((), (), s32[]{:S(2)}) async-start(), calls=%async_computation.2 | async-start | bytes 2359296 | tf_op jit(solution)/shard_map/all_gather | solution.py:33
  110.9 101.0 %all-reduce.6.cloned.1.call-start = ((), (), s32[]{:S(2)}) async-start(), calls=%async_computation.3 | async-start | bytes 1048576 | tf_op jit(solution)/shard_map/psum | solution.py:25
  177.3 1.3 copy-start
  180.1 83.7 %all-gather.8.cloned.1.call-start = ((), (), s32[]{:S(2)}) async-start(), calls=%async_computation.4 | async-start | bytes 2359296 | tf_op jit(solution)/shard_map/all_gather | solution.py:33
  214.3 98.8 %all-reduce.8.cloned.1.call-start = ((), (), s32[]{:S(2)}) async-start(), calls=%async_computation.5 | async-start | bytes 1048576 | tf_op jit(solution)/shard_map/psum | solution.py:25
  280.3 34.4 %copy-start.1 = (bf16[512,256]{1,0:T(8,128)(2,1)S(1)}, bf16[512,256]{1,0:T(8,128)(2,1)}, u32[]{:S(2)}) copy-start(bf16[512,256]{1,0:T(8,128)(2,1)} %convolution_convert_fusion.3) | copy-start | bytes 786436
  280.4 34.4 %copy-start.2 = (bf16[256,512]{0,1:T(8,128)(2,1)S(1)}, bf16[256,512]{0,1:T(8,128)(2,1)}, u32[]{:S(2)}) copy-start(bf16[256,512]{0,1:T(8,128)(2,1)} %convolution_convert_fusion.2) | copy-start | bytes 786436
  280.4 34.4 %copy-start.3 = (bf16[256,512]{0,1:T(8,128)(2,1)S(1)}, bf16[256,512]{0,1:T(8,128)(2,1)}, u32[]{:S(2)}) copy-start(bf16[256,512]{0,1:T(8,128)(2,1)} %convolution_convert_fusion.1) | copy-start | bytes 786436
Sparse Core Ops, SparseCore 0:
  9.5 51.9 all-gather.3
  76.8 31.6 all-reduce.3
  111.0 49.2 all-gather.5
  180.2 31.6 all-reduce.5
  214.4 49.2 all-gather.7
  281.3 31.6 all-reduce.7
where the time goes:
time: 323 us
  waiting for transfers between devices  245 us (76%)
  matrix products  32.5 us (10%)
  local copies, waits for them, and re-layouts  26.2 us (8%)
  between operations  13.6 us (4%)
  other arithmetic  4.63 us (1%)
    all_gather x3, waiting for transfers between devices, on_device(): gathered = lax.all_gather(solved, 'prow', axis=0, tiled=True)  150 us
    psum x3, waiting for transfers between devices, on_device(): summed = lax.psum(partial_value[tree_level], 'pcol')  95.5 us
    dot_general x3, matrix products, on_device(): jnp.einsum('tk,kxz->txz', indicator_matrix, block_products, precision=lax...  12.8 us
    dot_general x3, local copies, waits for them, and re-layouts, on_device(): jnp.einsum('bij,bjr->bir', lower_blocks[0, 0, tree_level], picked, prefer...  12.1 us
    dot_general x3, matrix products, on_device(): jnp.einsum('bij,bjr->bir', lower_blocks[0, 0, tree_level], picked, prefer...  11 us
  transfers between devices with their start and end apart: 6, of which 6 were waited for; matrix products, arithmetic and copies ran while one was open for 0% of the time, Pallas kernels for 0%

commit v1 on v0

--- a/solution.py
+++ b/solution.py
@@ -22,7 +22,9 @@
                 inverse, given_rhs.astype(jnp.bfloat16), preferred_element_type=jnp.float32
             ).astype(jnp.bfloat16)
         else:
-            summed = lax.psum(partial_value[tree_level], "pcol")
+            block = partial_value[tree_level]
+            parts = lax.all_gather(block, "pcol", axis=0, tiled=False)
+            summed = parts.sum(axis=0)
             solved = jnp.dot(
                 inverse,
                 (given_rhs - summed).astype(jnp.bfloat16),

time: 323 us -> 296 us (0.916)
  waiting for transfers between devices: 245 us -> 214 us
  other arithmetic: 4.63 us -> 9.99 us
    psum x3 -> x0, waiting for transfers between devices: 95.5 us -> none  [on_device(): summed = lax.psum(partial_value[tree_level], 'pcol')]
    all_gather x0 -> x3, waiting for transfers between devices: none -> 63.6 us  [on_device(): parts = lax.all_gather(block, 'pcol', axis=0, tiled=False)]
    reduce_sum x0 -> x3, other arithmetic: none -> 5.36 us  [on_device(): summed = parts.sum(axis=0)]
where the time goes in v1:
time: 296 us
  waiting for transfers between devices  214 us (72%)
  matrix products  32 us (11%)
  local copies, waits for them, and re-layouts  26.2 us (9%)
  between operations  13.6 us (5%)
  other arithmetic  9.99 us (3%)
    all_gather x3, waiting for transfers between devices, on_device(): gathered = lax.all_gather(solved, 'prow', axis=0, tiled=True)  150 us
    all_gather x3, waiting for transfers between devices, on_device(): parts = lax.all_gather(block, 'pcol', axis=0, tiled=False)  63.6 us
    dot_general x3, matrix products, on_device(): jnp.einsum('tk,kxz->txz', indicator_matrix, block_products, precision=lax...  12.8 us
    dot_general x3, local copies, waits for them, and re-layouts, on_device(): jnp.einsum('bij,bjr->bir', lower_blocks[0, 0, tree_level], picked, prefer...  12.1 us
    dot_general x3, matrix products, on_device(): jnp.einsum('bij,bjr->bir', lower_blocks[0, 0, tree_level], picked, prefer...  11 us
    dot_general x3, matrix products, on_device(): jnp.dot(inverse, (given_rhs - summed).astype(jnp.bfloat16), preferred_ele...  5.96 us
  transfers between devices with their start and end apart: 6, of which 6 were waited for; matrix products, arithmetic and copies ran while one was open for 0% of the time, Pallas kernels for 0%

profile of v1, /device:TPU:0, one launch (start us, length us, event | category | flops | bytes accessed | tf_op | source)
XLA Modules:
  0.0 295.8 jit_solution(4617689639271186889)
XLA Ops:
  6.5 0.0 all-gather.7.cloned.1.call-start
  6.5 2.2 convolution_convert_fusion.3
  8.8 0.0 all-gather.7.cloned.1.call-update
  8.8 0.0 all-gather.9.cloned.1.call-start
  8.8 0.7 compare_and_fusion
  9.5 0.7 slice_bitcast_fusion
  10.2 51.3 %all-gather.7.cloned.1.call-done = bf16[4096,256]{1,0:T(8,128)(2,1)} async-done(((bf16[512,256]{1,0:T(8,128)(2,1)}), bf16[4096,256]{1,0:T(8,128)(2,1)}) %all-gather.7.cloned.1.call-update) | async-done | bytes 2097168 | tf_op jit(solution)/shard_map/all_gather | solution.py:35
  61.5 1.1 dynamic-slice_bitcast_fusion.2
  62.6 1.8 gather_fusion
  64.4 3.2 %fusion.10 = f32[5,256,512]{2,1,0:T(8,128)S(1)} fusion(bf16[1,1,3,5,512,512]{5,4,3,2,1,0:T(8,128)(2,1)} %param.9, bf16[5,512,256]{2,1,0:T(8,128)(2,1)} %gather_fusion, pred[5]{0:T(512)(128)(4,1)S(1)} %get-tuple-element.15), kind=kOutput, calls=%fused_computation.13 | convolution fusion | flops 671744000 | bytes 6553605 | tf_op jit(solution)/shard_map/bij,bjr->bir/dot_general | solution.py:41
  67.5 3.5 %copy.15 = f32[5,256,512]{1,0,2:T(8,128)} copy(f32[5,256,512]{2,1,0:T(8,128)S(1)} %fusion.10) | data formatting | bytes 5242880 | tf_op jit(solution)/shard_map/bij,bjr->bir/dot_general | solution.py:41
  71.0 4.2 %fusion.4 = f32[4,512,256]{2,0,1:T(4,128)S(1)} fusion(f32[5,256,512]{1,0,2:T(8,128)} %copy.15, s32[5]{0:T(128)S(1)} %get-tuple-element.13), kind=kOutput, calls=%fused_computation.7 | convolution fusion | flops 31457300 | bytes 4718612 | tf_op jit(solution)/shard_map/tk,kxz->txz/dot_general | solution.py:50
  75.3 0.5 slice.88
  75.8 0.8 copy.9
  76.7 0.0 all-gather.9.cloned.1.call-update
  76.7 0.0 all-gather.11.cloned.1.call-start
  76.7 21.2 %all-gather.9.cloned.1.call-done = f32[4,512,256]{2,1,0:T(8,128)} async-done(((f32[1,512,256]{2,1,0:T(8,128)}), f32[4,512,256]{2,1,0:T(8,128)}) %all-gather.9.cloned.1.call-update) | async-done | bytes 2097168 | tf_op jit(solution)/shard_map/all_gather | solution.py:26
  97.9 1.8 reduce_sum.33
  99.7 2.2 convolution_convert_fusion.2
  101.9 0.0 all-gather.11.cloned.1.call-update
  102.0 0.0 all-gather.13.cloned.1.call-start
  102.0 49.4 %all-gather.11.cloned.1.call-done = bf16[4096,256]{1,0:T(8,128)(2,1)} async-done(((bf16[512,256]{1,0:T(8,128)(2,1)}), bf16[4096,256]{1,0:T(8,128)(2,1)}) %all-gather.11.cloned.1.call-update) | async-done | bytes 2097168 | tf_op jit(solution)/shard_map/all_gather | solution.py:35
  151.4 1.1 dynamic-slice_bitcast_fusion.1
  152.5 1.8 gather_fusion.1
  154.2 4.7 %fusion.8 = f32[5,256,512]{2,1,0:T(8,128)} fusion(bf16[1,1,3,5,512,512]{5,4,3,2,1,0:T(8,128)(2,1)} %param.9, bf16[5,512,256]{2,1,0:T(8,128)(2,1)} %gather_fusion.1, pred[5]{0:T(512)(128)(4,1)S(1)} %get-tuple-element.17), kind=kOutput, calls=%fused_computation.11 | convolution fusion | flops 671744000 | bytes 6553605 | tf_op jit(solution)/shard_map/bij,bjr->bir/dot_general | solution.py:41
  158.9 5.0 %copy.17 = f32[5,256,512]{1,0,2:T(8,128)} copy(f32[5,256,512]{2,1,0:T(8,128)} %fusion.8) | data formatting | bytes 5242880 | tf_op jit(solution)/shard_map/bij,bjr->bir/dot_general | solution.py:41
  164.0 4.4 %fusion.15 = f32[4,512,256]{2,0,1:T(4,128)S(1)} fusion(f32[4,512,256]{2,0,1:T(4,128)S(1)} %fusion.4, f32[5,256,512]{1,0,2:T(8,128)} %copy.17, s32[5]{0:T(128)S(1)} %get-tuple-element.14), kind=kOutput, calls=%fused_computation.18 | convolution fusion | flops 31981588 | bytes 6815764 | tf_op jit(solution)/shard_map/tk,kxz->txz/dot_general | solution.py:50
  168.3 0.0 copy-start
  168.4 1.3 copy-done
  169.7 0.5 slice.89
  170.2 0.8 copy.11
  171.1 0.0 all-gather.13.cloned.1.call-update
  171.1 0.0 all-gather.15.cloned.1.call-start
  171.1 21.2 %all-gather.13.cloned.1.call-done = f32[4,512,256]{2,1,0:T(8,128)} async-done(((f32[1,512,256]{2,1,0:T(8,128)}), f32[4,512,256]{2,1,0:T(8,128)}) %all-gather.13.cloned.1.call-update) | async-done | bytes 2097168 | tf_op jit(solution)/shard_map/all_gather | solution.py:26
  192.3 1.8 reduce_sum.35
  194.1 2.2 convolution_convert_fusion.1
  196.3 0.0 all-gather.15.cloned.1.call-update
  196.4 0.2 all-gather.17.cloned.1.call-start
  196.6 49.2 %all-gather.15.cloned.1.call-done = bf16[4096,256]{1,0:T(8,128)(2,1)} async-done(((bf16[512,256]{1,0:T(8,128)(2,1)}), bf16[4096,256]{1,0:T(8,128)(2,1)}) %all-gather.15.cloned.1.call-update) | async-done | bytes 2097168 | tf_op jit(solution)/shard_map/all_gather | solution.py:35
  245.8 1.1 dynamic-slice_bitcast_fusion
  246.9 1.8 gather_fusion.2
  248.7 3.2 %fusion.6 = f32[5,256,512]{2,1,0:T(8,128)S(1)} fusion(bf16[1,1,3,5,512,512]{5,4,3,2,1,0:T(8,128)(2,1)} %param.9, bf16[5,512,256]{2,1,0:T(8,128)(2,1)} %gather_fusion.2, pred[5]{0:T(512)(128)(4,1)S(1)} %get-tuple-element.6), kind=kOutput, calls=%fused_computation.9 | convolution fusion | flops 671744000 | bytes 6553605 | tf_op jit(solution)/shard_map/bij,bjr->bir/dot_general | solution.py:41
  251.8 3.5 %copy.19 = f32[5,256,512]{1,0,2:T(8,128)} copy(f32[5,256,512]{2,1,0:T(8,128)S(1)} %fusion.6) | data formatting | bytes 5242880 | tf_op jit(solution)/shard_map/bij,bjr->bir/dot_general | solution.py:41
  255.3 4.2 %fusion = f32[4,512,256]{2,0,1:T(4,128)S(1)} fusion(f32[5,256,512]{1,0,2:T(8,128)} %copy.19, s32[5]{0:T(128)S(1)} %get-tuple-element.12), kind=kOutput, calls=%fused_computation.3 | convolution fusion | flops 31457300 | bytes 4718612 | tf_op jit(solution)/shard_map/tk,kxz->txz/dot_general | solution.py:50
  259.6 2.8 slice_add_fusion
  262.4 0.8 copy.13
  263.2 0.0 all-gather.17.cloned.1.call-update
  263.2 0.0 copy-start.1
  263.2 0.0 copy-start.2
  263.2 0.0 copy-start.3
  263.3 21.2 %all-gather.17.cloned.1.call-done = f32[4,512,256]{2,1,0:T(8,128)} async-done(((f32[1,512,256]{2,1,0:T(8,128)}), f32[4,512,256]{2,1,0:T(8,128)}) %all-gather.17.cloned.1.call-update) | async-done | bytes 2097168 | tf_op jit(solution)/shard_map/all_gather | solution.py:26
  284.5 1.8 reduce_sum.37
  286.3 1.5 fusion.24
  287.8 0.0 copy-done.1
  287.8 0.0 copy-done.2
  287.8 0.0 copy-done.3
  287.8 1.1 maximum_bitcast_fusion
  (3 shorter events, 0.0 us)
Async XLA Ops:
  6.5 55.0 %all-gather.7.cloned.1.call-start = ((), (), s32[]{:S(2)}) async-start(), calls=%async_computation | async-start | bytes 2359296 | tf_op jit(solution)/shard_map/all_gather | solution.py:35
  8.8 89.1 %all-gather.9.cloned.1.call-start = ((), (), s32[]{:S(2)}) async-start(), calls=%async_computation.1 | async-start | bytes 2621440 | tf_op jit(solution)/shard_map/all_gather | solution.py:26
  76.7 74.7 %all-gather.11.cloned.1.call-start = ((), (), s32[]{:S(2)}) async-start(), calls=%async_computation.2 | async-start | bytes 2359296 | tf_op jit(solution)/shard_map/all_gather | solution.py:35
  102.0 90.4 %all-gather.13.cloned.1.call-start = ((), (), s32[]{:S(2)}) async-start(), calls=%async_computation.3 | async-start | bytes 2621440 | tf_op jit(solution)/shard_map/all_gather | solution.py:26
  168.3 1.3 copy-start
  171.1 74.7 %all-gather.15.cloned.1.call-start = ((), (), s32[]{:S(2)}) async-start(), calls=%async_computation.4 | async-start | bytes 2359296 | tf_op jit(solution)/shard_map/all_gather | solution.py:35
  196.4 88.1 %all-gather.17.cloned.1.call-start = ((), (), s32[]{:S(2)}) async-start(), calls=%async_computation.5 | async-start | bytes 2621440 | tf_op jit(solution)/shard_map/all_gather | solution.py:26
  263.2 24.6 %copy-start.1 = (bf16[512,256]{1,0:T(8,128)(2,1)S(1)}, bf16[512,256]{1,0:T(8,128)(2,1)}, u32[]{:S(2)}) copy-start(bf16[512,256]{1,0:T(8,128)(2,1)} %convolution_convert_fusion.3) | copy-start | bytes 786436
  263.2 24.6 %copy-start.2 = (bf16[256,512]{0,1:T(8,128)(2,1)S(1)}, bf16[256,512]{0,1:T(8,128)(2,1)}, u32[]{:S(2)}) copy-start(bf16[256,512]{0,1:T(8,128)(2,1)} %convolution_convert_fusion.2) | copy-start | bytes 786436
  263.2 24.6 %copy-start.3 = (bf16[256,512]{0,1:T(8,128)(2,1)S(1)}, bf16[256,512]{0,1:T(8,128)(2,1)}, u32[]{:S(2)}) copy-start(bf16[256,512]{0,1:T(8,128)(2,1)} %convolution_convert_fusion.1) | copy-start | bytes 786436
Sparse Core Ops, SparseCore 0:
  9.5 51.9 all-gather.6
  76.8 21.0 all-gather.8
  102.1 49.2 all-gather.10
  171.2 21.0 all-gather.12
  196.5 49.2 all-gather.14
  263.4 21.0 all-gather.16
